TPU v7x, 128 devices: a whole 4x4x4 slice. The times are simulated.
128 devices in a mesh: row: 8 (over z_hi, x), col: 16 (over y, z_lo, core).
Axes of the slice: x: 4, y: 4, z: 4 (z_hi: 2, z_lo: 2; z = z_hi * 2 + z_lo), core: 2. Of those that a mesh axis runs over, the one named last changes fastest.
Arguments:
- features: bfloat16 [320, 320, 2048], P('row', 'col'), may hold values from 0 to 30
- w_point: bfloat16 [2048, 128], replicated, may hold values from -0.125 to 0.125
- w_rate_six: bfloat16 [3, 3, 2048, 128], replicated, may hold values from -0.046875 to 0.046875
- w_rate_twelve: bfloat16 [3, 3, 2048, 128], replicated, may hold values from -0.046875 to 0.046875
- w_rate_eighteen: bfloat16 [3, 3, 2048, 128], replicated, may hold values from -0.046875 to 0.046875
- w_pool: bfloat16 [2048, 128], replicated, may hold values from -0.125 to 0.125
- w_proj: bfloat16 [640, 256], replicated, may hold values from -0.25 to 0.25
Outputs:
- head_out: bfloat16 [320, 320, 256], P('row', 'col')
All inputs are finite; a program needn't handle non-finite values.
Results may differ from a plain program's by a relative error of at most 0.0052.
Values may be sent and summed in bfloat16 or wider, within the bound.
A program may use at most 192 MiB of HBM per device.

v0:
```python
import jax
import jax.numpy as jnp
from jax import lax
from jax.sharding import PartitionSpec as P


def padded_2(cells, sides, width):
    for axis, dim in sides:
        count = lax.axis_size(axis)
        ends = count - 1
        head = lax.slice_in_dim(cells, 0, width, axis=dim)
        tail = lax.slice_in_dim(cells, cells.shape[dim] - width, cells.shape[dim], axis=dim)
        cells = jnp.concatenate(
            [
                lax.ppermute(tail, axis, [(i, (i + 1) % count) for i in range(ends)]),
                cells,
                lax.ppermute(head, axis, [((i + 1) % count, i) for i in range(ends)]),
            ],
            axis=dim,
        )
    return cells


def per_device(features, w_point, w_rate_six, w_rate_twelve, w_rate_eighteen, w_pool, w_proj):
    tile_rows, tile_cols, chans = features.shape
    width = w_point.shape[1]
    rates = (6, 12, 18)
    kernels = (w_rate_six, w_rate_twelve, w_rate_eighteen)
    local_sum = jnp.sum(features, axis=(0, 1), dtype=jnp.float32)
    total = lax.psum(local_sum, ("row", "col"))
    count = tile_rows * lax.axis_size("row") * tile_cols * lax.axis_size("col")
    pooled = (total / count).astype(jnp.bfloat16)
    pool_branch = jax.nn.relu(
        jnp.dot(pooled[None], w_pool, preferred_element_type=jnp.float32)
    ).astype(jnp.bfloat16)
    point_branch = jax.nn.relu(
        jnp.einsum("rcf,fo->rco", features, w_point, preferred_element_type=jnp.float32)
    ).astype(jnp.bfloat16)
    branches = [point_branch]
    reach = max(rates)
    padded = padded_2(features, (("row", 0), ("col", 1)), reach)
    for rate, kernel in zip(rates, kernels):
        summed = jnp.zeros((tile_rows, tile_cols, width), jnp.float32)
        for tap_row in range(3):
            for tap_col in range(3):
                top = reach + (tap_row - 1) * rate
                left = reach + (tap_col - 1) * rate
                window = padded[top : top + tile_rows, left : left + tile_cols]
                summed = summed + jnp.einsum(
                    "rcf,fo->rco",
                    window,
                    kernel[tap_row, tap_col],
                    preferred_element_type=jnp.float32,
                )
        branches.append(jax.nn.relu(summed).astype(jnp.bfloat16))
    branches.append(jnp.broadcast_to(pool_branch[None], (tile_rows, tile_cols, width)))
    joined = jnp.concatenate(branches, axis=-1)
    mixed = jnp.einsum("rck,ko->rco", joined, w_proj, preferred_element_type=jnp.float32)
    return jax.nn.relu(mixed).astype(jnp.bfloat16)


def solution(mesh):
    placed = (P("row", "col", None), P(), P(), P(), P(), P(), P())
    return jax.shard_map(
        per_device, mesh=mesh, in_specs=placed, out_specs=P("row", "col", None), check_vma=False
    )
```

profile of v0, /device:TPU:1, one launch (start us, length us, event | category | flops | bytes accessed | tf_op | source)
XLA Modules:
  0.0 344.2 jit_solution(6274292249092239310)
XLA Ops:
  0.0 3.0 fusion.217
  3.9 4.2 %collective-permute-start = (bf16[18,20,2048]{2,1,0:T(8,128)(2,1)S(1)}, bf16[18,20,2048]{2,1,0:T(8,128)(2,1)S(1)}, u32[]{:S(2)}, u32[]{:S(2)}) collective-permute-start(bf16[18,20,2048]{2,1,0:T(8,128)(2,1)S(1)} %copy.14), channel_id=1, source_target_pairs={{0,16},{16,32},{32,48},{48,64},{64,80},{80,96},{96,112},{1,17},{17... | collective-permute-start | bytes 4423688 | tf_op jit(solution)/shard_map/ppermute | solution.py:15
  10.6 34.6 %collective-permute-done = bf16[18,20,2048]{2,1,0:T(8,128)(2,1)S(1)} collective-permute-done((bf16[18,20,2048]{2,1,0:T(8,128)(2,1)S(1)}, bf16[18,20,2048]{2,1,0:T(8,128)(2,1)S(1)}, u32[]{:S(2)}, u32[]{:S(2)}) %collective-permute-start) | collective-permute-done | bytes 1474592 | tf_op jit(solution)/shard_map/ppermute | solution.py:15
  46.1 3.9 %collective-permute-done.1 = bf16[18,20,2048]{2,1,0:T(8,128)(2,1)S(1)} collective-permute-done((bf16[18,20,2048]{2,1,0:T(8,128)(2,1)S(1)}, bf16[18,20,2048]{2,1,0:T(8,128)(2,1)S(1)}, u32[]{:S(2)}, u32[]{:S(2)}) %collective-permute-start.1) | collective-permute-done | bytes 1474592 | tf_op jit(solution)/shard_map/ppermute | solution.py:17
  50.9 2.3 copy-done.8
  54.4 2.6 pad_maximum_fusion.1
  57.0 4.7 %fusion.216 = (bf16[76,18,2048]{2,0,1:T(8,128)(2,1)}, bf16[76,18,2048]{2,0,1:T(8,128)(2,1)}) fusion(bf16[76,20,2048]{2,0,1:T(8,128)(2,1)S(1)} %pad_maximum_fusion.1), kind=kLoop, calls=%fused_computation.164 | loop fusion | bytes 22413312 | tf_op jit(solution)/shard_map/slice | solution.py:12
  61.8 5.3 %collective-permute-start.2 = (bf16[76,18,2048]{2,0,1:T(8,128)(2,1)}, bf16[76,18,2048]{2,0,1:T(8,128)(2,1)}, u32[]{:S(2)}, u32[]{:S(2)}) collective-permute-start(bf16[76,18,2048]{2,0,1:T(8,128)(2,1)} %get-tuple-element.7), channel_id=1, source_target_pairs={{0,1},{1,2},{2,3},{3,4},{4,5},{5,6},{6,7},{7,8},{8,9},{9,10},{10,1... | collective-permute-start | bytes 16809992 | tf_op jit(solution)/shard_map/ppermute | solution.py:15
  67.1 2.3 collective-permute-start.3
  69.9 187.9 %psum.7 = f32[2048]{0:T(1024)S(1)} all-reduce(f32[2048]{0:T(1024)S(1)} %convert_reduce_fusion), channel_id=1, replica_groups=mesh['row'=8,'col'=16] {'row','col'}, use_global_device_ids=true, to_apply=%region_1.0 | all-reduce | flops 2048 | bytes 16384 | tf_op jit(solution)/shard_map/psum | solution.py:30
  258.1 3.8 %fusion.133 = bf16[40,20,640]{2,0,1:T(8,128)(2,1)} fusion(bf16[40,20,2048]{2,0,1:T(8,128)(2,1)} %param.7, bf16[2048,128]{1,0:T(8,128)(2,1)S(1)} %copy-done), kind=kOutput, calls=%fused_computation.88 | convolution fusion | flops 419635200 | bytes 4005888 | tf_op jit(solution)/shard_map/rcf,fo->rco/dot_general | solution.py:37
  264.1 3.0 fusion.168
  271.4 3.5 %fusion.46 = f32[40,20,128]{2,0,1:T(8,128)} fusion(bf16[40,20,2048]{2,0,1:T(8,128)(2,1)S(1)} %copy-done.3, bf16[18,20,2048]{2,0,1:T(8,128)(2,1)S(1)} %copy-done.6, bf16[3,3,2048,128]{3,2,1,0:T(8,128)(2,1)} %param.9), kind=kOutput, calls=%fused_computation.55 | convolution fusion | flops 425984000 | bytes 5685248 | tf_op jit(solution)/shard_map/rcf,fo->rco/dot_general | solution.py:49
  274.9 3.4 fusion.48
  278.2 2.2 fusion.4
  280.4 3.0 fusion.20
  283.4 3.0 fusion.34
  286.4 20.8 %maximum_maximum_fusion = (bf16[76,38,2048]{2,0,1:T(8,128)(2,1)}, bf16[76,38,2048]{2,0,1:T(8,128)(2,1)}) fusion(bf16[18,20,2048]{2,0,1:T(8,128)(2,1)} %copy-done.7, bf16[40,20,2048]{2,0,1:T(8,128)(2,1)S(1)} %copy-done.3, bf16[18,20,2048]{2,0,1:T(8,128)(2,1)} %copy-done.5, bf16[76,18,2048]{2,0,1:T(8,128)(2,1)} %collective-permute-done.2, ...), kind=kLoop, calls=%fused_computation | loop fusion | flops 94633984 | bytes 41091072 | tf_op jit(solution)/shard_map/concatenate | solution.py:13
  307.2 3.5 %fusion.6 = f32[40,20,128]{2,0,1:T(8,128)S(1)} fusion(bf16[76,38,2048]{2,0,1:T(8,128)(2,1)} %get-tuple-element.5, bf16[3,3,2048,128]{3,2,1,0:T(8,128)(2,1)} %param.11), kind=kOutput, calls=%fused_computation.14 | convolution fusion | flops 419430400 | bytes 4210688 | tf_op jit(solution)/shard_map/rcf,fo->rco/dot_general | solution.py:49
  310.8 4.2 %fusion.10 = f32[40,20,128]{2,0,1:T(8,128)S(1)} fusion(bf16[76,38,2048]{2,0,1:T(8,128)(2,1)} %get-tuple-element.5, bf16[3,3,2048,128]{3,2,1,0:T(8,128)(2,1)} %param.11), kind=kOutput, calls=%fused_computation.18 | convolution fusion | flops 419430400 | bytes 4210688 | tf_op jit(solution)/shard_map/rcf,fo->rco/dot_general | solution.py:49
  315.0 3.0 fusion.22
  322.9 2.2 fusion.2
  325.1 2.2 fusion.8
  340.1 2.3 fusion.143
  (84 shorter events, 32.2 us)
Async XLA Ops:
  0.0 258.1 %copy-start = (bf16[2048,128]{1,0:T(8,128)(2,1)S(1)}, bf16[2048,128]{1,0:T(8,128)(2,1)}, u32[]{:S(2)}) copy-start(bf16[2048,128]{1,0:T(8,128)(2,1)} %param.8) | copy-start | bytes 1572868
  3.0 7.2 %copy-start.2 = (bf16[40,20,2048]{2,0,1:T(8,128)(2,1)S(1)}, bf16[40,20,2048]{2,0,1:T(8,128)(2,1)}, u32[]{:S(2)}) copy-start(bf16[40,20,2048]{2,0,1:T(8,128)(2,1)} %param.7) | copy-start | bytes 9830404
  3.9 41.3 %collective-permute-start = (bf16[18,20,2048]{2,1,0:T(8,128)(2,1)S(1)}, bf16[18,20,2048]{2,1,0:T(8,128)(2,1)S(1)}, u32[]{:S(2)}, u32[]{:S(2)}) collective-permute-start(bf16[18,20,2048]{2,1,0:T(8,128)(2,1)S(1)} %copy.14), channel_id=1, source_target_pairs={{0,16},{16,32},{32,48},{48,64},{64,80},{80,96},{96,112},{1,17},{17... | collective-permute-start | bytes 4423688 | tf_op jit(solution)/shard_map/ppermute | solution.py:15
  8.9 41.1 %collective-permute-start.1 = (bf16[18,20,2048]{2,1,0:T(8,128)(2,1)S(1)}, bf16[18,20,2048]{2,1,0:T(8,128)(2,1)S(1)}, u32[]{:S(2)}, u32[]{:S(2)}) collective-permute-start(bf16[18,20,2048]{2,1,0:T(8,128)(2,1)S(1)} %copy.15), channel_id=1, source_target_pairs={{16,0},{32,16},{48,32},{64,48},{80,64},{96,80},{112,96},{17,1},{33... | collective-permute-start | bytes 4423688 | tf_op jit(solution)/shard_map/ppermute | solution.py:17
  46.0 7.1 %copy-start.5 = (bf16[18,20,2048]{2,0,1:T(8,128)(2,1)}, bf16[18,20,2048]{2,0,1:T(8,128)(2,1)S(1)}, u32[]{:S(2)}) copy-start(bf16[18,20,2048]{2,0,1:T(8,128)(2,1)S(1)} %copy.10) | copy-start | bytes 4423684
  50.9 2.3 copy-start.8
  57.0 200.8 %copy-start.9 = (bf16[2048,128]{1,0:T(8,128)(2,1)S(1)}, bf16[2048,128]{1,0:T(8,128)(2,1)}, u32[]{:S(2)}) copy-start(bf16[2048,128]{1,0:T(8,128)(2,1)} %param.12) | copy-start | bytes 1572868
  61.8 224.6 %collective-permute-start.2 = (bf16[76,18,2048]{2,0,1:T(8,128)(2,1)}, bf16[76,18,2048]{2,0,1:T(8,128)(2,1)}, u32[]{:S(2)}, u32[]{:S(2)}) collective-permute-start(bf16[76,18,2048]{2,0,1:T(8,128)(2,1)} %get-tuple-element.7), channel_id=1, source_target_pairs={{0,1},{1,2},{2,3},{3,4},{4,5},{5,6},{6,7},{7,8},{8,9},{9,10},{10,1... | collective-permute-start | bytes 16809992 | tf_op jit(solution)/shard_map/ppermute | solution.py:15
  67.1 219.3 %collective-permute-start.3 = (bf16[76,18,2048]{2,0,1:T(8,128)(2,1)}, bf16[76,18,2048]{2,0,1:T(8,128)(2,1)}, u32[]{:S(2)}, u32[]{:S(2)}) collective-permute-start(bf16[76,18,2048]{2,0,1:T(8,128)(2,1)} %get-tuple-element.8), channel_id=1, source_target_pairs={{1,0},{2,1},{3,2},{4,3},{5,4},{6,5},{7,6},{8,7},{9,8},{10,9},{11,1... | collective-permute-start | bytes 16809992 | tf_op jit(solution)/shard_map/ppermute | solution.py:17
  257.9 4.1 %copy-start.3 = (bf16[40,20,2048]{2,0,1:T(8,128)(2,1)S(1)}, bf16[40,20,2048]{2,0,1:T(8,128)(2,1)}, u32[]{:S(2)}) copy-start(bf16[40,20,2048]{2,0,1:T(8,128)(2,1)} %param.7) | copy-start | bytes 9830404
  264.0 5.2 %copy-start.6 = (bf16[18,20,2048]{2,0,1:T(8,128)(2,1)S(1)}, bf16[18,20,2048]{2,0,1:T(8,128)(2,1)}, u32[]{:S(2)}) copy-start(bf16[18,20,2048]{2,0,1:T(8,128)(2,1)} %copy-done.5) | copy-start | bytes 4423684
  271.4 6.8 %slice-start.3 = ((s8[5242880]{0:T(1024)(128)(4,1)}), s8[4194304]{0:T(1024)(128)(4,1)S(1)}, s32[]{:S(2)}) async-start(s8[5242880]{0:T(1024)(128)(4,1)} %bitcast.156), calls=%async_computation.3 | async-start | bytes 8388608
  274.9 3.4 slice-start.4
  307.2 7.7 %copy-start.4 = (bf16[76,38,2048]{2,0,1:T(8,128)(2,1)S(1)}, bf16[76,38,2048]{2,0,1:T(8,128)(2,1)}, u32[]{:S(2)}) copy-start(bf16[76,38,2048]{2,0,1:T(8,128)(2,1)} %get-tuple-element.5) | copy-start | bytes 35487748
  310.8 7.3 %slice-start.7 = ((s8[4718592]{0:T(1024)(128)(4,1)}), s8[4194304]{0:T(1024)(128)(4,1)S(1)}, s32[]{:S(2)}) async-start(s8[4718592]{0:T(1024)(128)(4,1)} %bitcast.160), calls=%async_computation.7 | async-start | bytes 8388608
  310.8 8.5 %slice-start.5 = ((s8[4718592]{0:T(1024)(128)(4,1)}), s8[4194304]{0:T(1024)(128)(4,1)S(1)}, s32[]{:S(2)}) async-start(s8[4718592]{0:T(1024)(128)(4,1)} %bitcast.158), calls=%async_computation.5 | async-start | bytes 8388608
  315.0 3.1 slice-start.8
  315.0 4.3 %slice-start.6 = ((s8[4718592]{0:T(1024)(128)(4,1)}), s8[524288]{0:T(1024)(128)(4,1)S(1)}, s32[]{:S(2)}) async-start(s8[4718592]{0:T(1024)(128)(4,1)} %bitcast.158), calls=%async_computation.6 | async-start | bytes 1048576
  318.1 3.5 %slice-start = ((s8[12451840]{0:T(1024)(128)(4,1)}), s8[4194304]{0:T(1024)(128)(4,1)S(1)}, s32[]{:S(2)}) async-start(s8[12451840]{0:T(1024)(128)(4,1)} %bitcast.154), calls=%async_computation | async-start | bytes 8388608
  318.1 3.5 %slice-start.1 = ((s8[12451840]{0:T(1024)(128)(4,1)}), s8[4194304]{0:T(1024)(128)(4,1)S(1)}, s32[]{:S(2)}) async-start(s8[12451840]{0:T(1024)(128)(4,1)} %bitcast.154), calls=%async_computation.1 | async-start | bytes 8388608
  320.4 2.5 slice-start.2
  335.8 1.4 copy-start.10
  338.7 5.1 %copy-start.1 = (bf16[2048,128]{1,0:T(8,128)(2,1)S(1)}, bf16[2048,128]{1,0:T(8,128)(2,1)}, u32[]{:S(2)}) copy-start(bf16[2048,128]{1,0:T(8,128)(2,1)} %param.8) | copy-start | bytes 1572868
  340.1 2.4 copy-start.11
  (6 other events, 7.9 us)
where the time goes:
time: 350 us; the launch traced here: 344 us
  blocking collectives  188 us (54%)
  matrix products  63.1 us (18%)
  waiting for transfers between devices  38.4 us (11%)
  other arithmetic  24 us (7%)
  local copies, waits for them, and re-layouts  16.6 us (5%)
  starting transfers between devices  13.1 us (4%)
    psum x1, blocking collectives, per_device(): total = lax.psum(local_sum, ('row', 'col'))  188 us
    dot_general x27, matrix products, per_device(): jnp.einsum('rcf,fo->rco', window, kernel[tap_row, tap_col], preferred_ele...  57.9 us
    ppermute x2, waiting for transfers between devices, padded_2(): lax.ppermute(tail, axis, [(i, (i + 1) % count) for i in range(ends)])  34.6 us
    concatenate x2, other arithmetic, padded_2(): jnp.concatenate([lax.ppermute(tail, axis, [(i, (i + 1) % count) for i in...  23.4 us
    ppermute x2, starting transfers between devices, padded_2(): lax.ppermute(tail, axis, [(i, (i + 1) % count) for i in range(ends)])  9.47 us
    slice x2, local copies, waits for them, and re-layouts, padded_2(): lax.slice_in_dim(cells, cells.shape[dim] - width, cells.shape[dim], axis=...  7.72 us
    unnamed x55, local copies, waits for them, and re-layouts  7.05 us
  transfers between devices with their start and end apart: 4, of which 2 were waited for; matrix products, arithmetic and copies ran while one was open for 9% of the time, Pallas kernels for 0%

commit v1 on v0

v1 whole, which is shorter than its diff:
```python
import functools

import jax
import jax.numpy as jnp
from jax import lax
from jax.experimental import pallas as pl
from jax.experimental.pallas import tpu as pltpu
from jax.sharding import PartitionSpec as P

MESH = pl.DeviceIdType.MESH
BF = jnp.bfloat16
F32 = jnp.float32
RATES = (18, 12, 6)
ROWS, COLS, BR, OUT = 40, 20, 128, 256
PIX = ROWS * COLS
GROUP = 8
SPAN = GROUP * COLS


def up16(n):
    return -(-n // 16) * 16


def body(
    n_row, n_col,
    x_hbm, wp_hbm, w6_hbm, w12_hbm, w18_hbm, wpool_hbm, wproj_hbm,
    out_ref,
    xraw, xc, w18, w12, w6, wp, wpool, wproj,
    z18, z12, z6, point,
    su18, su12, su6, sd18, sd12, sd6, ru18, ru12, ru6, rd18, rd12, rd6,
    sl18, sl12, sl6, sr18, sr12, sr6, rl18, rl12, rl6, rr18, rr12, rr6,
    psum, prow, pcol, poolrow,
    xsem, wsem, wsem2, row_ss, row_rs, col_ss, col_rs, pr_ss, pr_rs, pc_ss, pc_rs,
):
    r = lax.axis_index("row")
    c = lax.axis_index("col")
    has_up, has_down = r > 0, r < n_row - 1
    has_left, has_right = c > 0, c < n_col - 1
    up, down = lax.rem(r + n_row - 1, n_row), lax.rem(r + 1, n_row)
    left, right = lax.rem(c + n_col - 1, n_col), lax.rem(c + 1, n_col)

    W = {18: w18, 12: w12, 6: w6}
    Z = {18: z18, 12: z12, 6: z6}
    SU, SD = {18: su18, 12: su12, 6: su6}, {18: sd18, 12: sd12, 6: sd6}
    RU, RD = {18: ru18, 12: ru12, 6: ru6}, {18: rd18, 12: rd12, 6: rd6}
    SL, SR = {18: sl18, 12: sl12, 6: sl6}, {18: sr18, 12: sr12, 6: sr6}
    RL, RR = {18: rl18, 12: rl12, 6: rl6}, {18: rr18, 12: rr12, 6: rr6}

    xcopies = []
    for i in range(5):
        cp = pltpu.make_async_copy(x_hbm.at[pl.ds(8 * i, 8)], xraw.at[pl.ds(8 * i, 8)], xsem.at[i])
        cp.start()
        xcopies.append(cp)
    wcopies = {}
    for n, (d, hbm) in enumerate(((18, w18_hbm), (12, w12_hbm), (6, w6_hbm))):
        for m, a in enumerate((0, 2, 1)):
            cp = pltpu.make_async_copy(hbm.at[a], W[d].at[a], wsem.at[3 * n + m])
            cp.start()
            wcopies[d, a] = cp
    tail = []
    for i, (s, t) in enumerate(((wp_hbm, wp), (wpool_hbm, wpool), (wproj_hbm, wproj))):
        cp = pltpu.make_async_copy(s, t, wsem2.at[i])
        cp.start()
        tail.append(cp)

    barrier = pltpu.get_barrier_semaphore()
    for k in range(1, n_row):
        pl.semaphore_signal(barrier, inc=1, device_id=(lax.rem(r + k, n_row), c), device_id_type=MESH)
    for k in range(1, n_col):
        pl.semaphore_signal(barrier, inc=1, device_id=(r, lax.rem(c + k, n_col)), device_id_type=MESH)

    psum[...] = jnp.zeros_like(psum)
    for i in range(5):
        xcopies[i].wait()
        for h in range(2):
            rows = [xraw[8 * i + 4 * h + k].astype(F32) for k in range(4)]
            flat = jnp.concatenate(rows, axis=0)
            n = 4 * COLS
            base = (2 * i + h) * n
            xc[base : base + n] = flat.astype(BF)
            part = flat[0:8]
            for k in range(1, n // 8):
                part = part + flat[8 * k : 8 * k + 8]
            psum[...] += part

    chans = xc.shape[1]
    lanes = chans // BR
    total = jnp.sum(psum[...], axis=0, keepdims=True)
    prow[0] = jnp.concatenate([total[:, BR * k : BR * k + BR] for k in range(lanes)], axis=0)
    pl.semaphore_wait(barrier, n_row + n_col - 2)

    def pool_row(k):
        return pltpu.make_async_remote_copy(
            src_ref=prow.at[0], dst_ref=prow.at[k], send_sem=pr_ss.at[k], recv_sem=pr_rs.at[k],
            device_id=(lax.rem(r + k, n_row), c), device_id_type=MESH)

    def pool_col(k):
        return pltpu.make_async_remote_copy(
            src_ref=pcol.at[0], dst_ref=pcol.at[k], send_sem=pc_ss.at[k], recv_sem=pc_rs.at[k],
            device_id=(r, lax.rem(c + k, n_col)), device_id_type=MESH)

    for k in range(1, n_row):
        pool_row(k).start()

    def row_copy(d, way):
        n = 2 * RATES.index(d) + way
        src, dst, to = ((SU[d], RU[d], up), (SD[d], RD[d], down))[way]
        return pltpu.make_async_remote_copy(
            src_ref=src, dst_ref=dst, send_sem=row_ss.at[n], recv_sem=row_rs.at[n],
            device_id=(to, c), device_id_type=MESH)

    def col_copy(d, way):
        n = 2 * RATES.index(d) + way
        src, dst, to = ((SL[d], RR[d], left), (SR[d], RL[d], right))[way]
        return pltpu.make_async_remote_copy(
            src_ref=src, dst_ref=dst, send_sem=col_ss.at[n], recv_sem=col_rs.at[n],
            device_id=(r, to), device_id_type=MESH)

    def dot2(wa, wb):
        w = jnp.concatenate([wa, wb], axis=1)
        y = jnp.dot(xc[...], w, preferred_element_type=F32)
        return y[:, :BR], y[:, BR:]

    def off_rows(d):
        w, z = W[d], Z[d]
        edge = 2 * d * COLS
        for b in range(3):
            down_part, up_part = dot2(w[0, b], w[2, b])
            z[b, 0:PIX] = up_part
            z[b, edge:PIX] += down_part[0 : PIX - edge]
            z[b, PIX : PIX + edge] = down_part[PIX - edge : PIX]
        high = up16(d * COLS)
        size = z.shape[1]
        SU[d][...] = z[:, 0:high].astype(BF)
        SD[d][...] = z[:, size - high : size].astype(BF)

        @pl.when(has_up)
        def _():
            row_copy(d, 0).start()

        @pl.when(has_down)
        def _():
            row_copy(d, 1).start()

    def own_rows(d):
        w, z = W[d], Z[d]
        y0, y2 = dot2(w[1, 0], w[1, 2])
        z[0, d * COLS : d * COLS + PIX] += y0
        z[2, d * COLS : d * COLS + PIX] += y2

    def rows_in(d):
        z = Z[d]
        n = d * COLS
        gap = up16(n) - n

        @pl.when(has_down)
        def _():
            row_copy(d, 0).wait_recv()
            for b in range(3):
                z[b, PIX : PIX + n] += RU[d][b].astype(F32)[0:n]

        @pl.when(has_up)
        def _():
            row_copy(d, 1).wait_recv()
            for b in range(3):
                z[b, n : 2 * n] += RD[d][b].astype(F32)[gap : gap + n]

    def cols_out(d):
        z = Z[d]
        for i in range(ROWS // GROUP):
            at = d * COLS + i * SPAN
            z0 = z[0, at : at + SPAN]
            z2 = z[2, at : at + SPAN]
            SR[d][i * GROUP * d : (i + 1) * GROUP * d] = jnp.concatenate(
                [z0[COLS * k + COLS - d : COLS * k + COLS] for k in range(GROUP)], axis=0).astype(BF)
            SL[d][i * GROUP * d : (i + 1) * GROUP * d] = jnp.concatenate(
                [z2[COLS * k : COLS * k + d] for k in range(GROUP)], axis=0).astype(BF)

        @pl.when(has_left)
        def _():
            col_copy(d, 0).start()

        @pl.when(has_right)
        def _():
            col_copy(d, 1).start()

    @pl.when(jnp.logical_not(has_left))
    def _():
        for d in RATES:
            RL[d][...] = jnp.zeros_like(RL[d])

    @pl.when(jnp.logical_not(has_right))
    def _():
        for d in RATES:
            RR[d][...] = jnp.zeros_like(RR[d])

    wcopies[18, 0].wait()
    wcopies[18, 2].wait()
    off_rows(18)
    wcopies[18, 1].wait()
    own_rows(18)
    wcopies[12, 0].wait()
    wcopies[12, 2].wait()
    off_rows(12)
    rows_in(18)
    cols_out(18)
    wcopies[12, 1].wait()
    own_rows(12)

    for k in range(1, n_row):
        pool_row(k).wait_recv()
    acc = prow[0]
    for k in range(1, n_row):
        acc = acc + prow[k]
    pcol[0] = acc
    for k in range(1, n_col):
        pool_col(k).start()

    wcopies[6, 0].wait()
    wcopies[6, 2].wait()
    off_rows(6)
    rows_in(12)
    cols_out(12)
    wcopies[6, 1].wait()
    own_rows(6)
    y18, y12 = dot2(w18[1, 1], w12[1, 1])
    z18[1, 18 * COLS : 18 * COLS + PIX] += y18
    z12[1, 12 * COLS : 12 * COLS + PIX] += y12
    rows_in(6)
    cols_out(6)
    for cp in tail:
        cp.wait()
    y6, yp = dot2(w6[1, 1], wp[...])
    z6[1, 6 * COLS : 6 * COLS + PIX] += y6
    point[...] = jnp.maximum(yp, 0.0).astype(BF)

    for k in range(1, n_col):
        pool_col(k).wait_recv()
    acc = pcol[0]
    for k in range(1, n_col):
        acc = acc + pcol[k]
    pooled = (acc / (PIX * n_row * n_col)).astype(BF).astype(F32)
    flat = jnp.concatenate([pooled[k : k + 1] for k in range(lanes)], axis=1)
    flat = jnp.broadcast_to(flat, (16, chans)).astype(BF)
    branch = jnp.maximum(jnp.dot(flat, wpool[...], preferred_element_type=F32), 0.0).astype(BF)
    poolrow[...] = jnp.dot(branch, wproj[4 * BR : 5 * BR], preferred_element_type=F32)[0:8]

    for d in RATES:
        @pl.when(has_right)
        def _(d=d):
            col_copy(d, 0).wait_recv()

        @pl.when(has_left)
        def _(d=d):
            col_copy(d, 1).wait_recv()

    base_row = poolrow[0:1]
    for i in range(ROWS // GROUP):
        at = i * SPAN
        joined = [point[at : at + SPAN]]
        for d in (6, 12, 18):
            z = Z[d]
            z0, z1, z2 = (z[b, d * COLS + at : d * COLS + at + SPAN] for b in range(3))
            got_l = RL[d][i * GROUP * d : (i + 1) * GROUP * d].astype(F32)
            got_r = RR[d][i * GROUP * d : (i + 1) * GROUP * d].astype(F32)
            from_left, from_right = [], []
            for k in range(GROUP):
                from_left += [got_l[k * d : (k + 1) * d], z0[COLS * k : COLS * k + COLS - d]]
                from_right += [z2[COLS * k + d : COLS * k + COLS], got_r[k * d : (k + 1) * d]]
            whole = z1 + jnp.concatenate(from_left, axis=0) + jnp.concatenate(from_right, axis=0)
            joined.append(jnp.maximum(whole, 0.0).astype(BF))
        mixed = jnp.dot(jnp.concatenate(joined, axis=1), wproj[0 : 4 * BR], preferred_element_type=F32)
        out_ref[at : at + SPAN] = jnp.maximum(mixed + base_row, 0.0).astype(BF)

    for k in range(1, n_row):
        pool_row(k).wait_send()
    for k in range(1, n_col):
        pool_col(k).wait_send()
    for d in RATES:
        @pl.when(has_up)
        def _(d=d):
            row_copy(d, 0).wait_send()

        @pl.when(has_down)
        def _(d=d):
            row_copy(d, 1).wait_send()

        @pl.when(has_left)
        def _(d=d):
            col_copy(d, 0).wait_send()

        @pl.when(has_right)
        def _(d=d):
            col_copy(d, 1).wait_send()


def per_device(n_row, n_col, features, w_point, w_rate_six, w_rate_twelve, w_rate_eighteen, w_pool, w_proj):
    chans = features.shape[2]
    lanes = chans // BR
    vm = pltpu.VMEM
    dma = pltpu.SemaphoreType.DMA
    scratch = [vm((ROWS, COLS, chans), BF), vm((PIX, chans), BF)]
    scratch += [vm((3, 3, chans, BR), BF)] * 3
    scratch += [vm((chans, BR), BF), vm((chans, BR), BF), vm((5 * BR, OUT), BF)]
    scratch += [vm((3, PIX + 2 * d * COLS, BR), F32) for d in RATES]
    scratch += [vm((PIX, BR), BF)]
    for _ in range(4):
        scratch += [vm((3, up16(d * COLS), BR), BF) for d in RATES]
    for _ in range(4):
        scratch += [vm((ROWS * d, BR), BF) for d in RATES]
    scratch += [vm((8, chans), F32), vm((n_row, lanes, BR), F32), vm((n_col, lanes, BR), F32), vm((8, OUT), F32)]
    scratch += [dma((5,)), dma((9,)), dma((3,)), dma((6,)), dma((6,)), dma((6,)), dma((6,)),
                dma((n_row,)), dma((n_row,)), dma((n_col,)), dma((n_col,))]
    flops = 2 * PIX * chans * BR * 28 + 2 * PIX * 5 * BR * OUT
    out = pl.pallas_call(
        functools.partial(body, n_row, n_col),
        name="aspp_head",
        out_shape=jax.ShapeDtypeStruct((PIX, OUT), BF),
        in_specs=[pl.BlockSpec(memory_space=pl.ANY)] * 7,
        out_specs=pl.BlockSpec(memory_space=pltpu.VMEM),
        scratch_shapes=scratch,
        compiler_params=pltpu.CompilerParams(
            collective_id=0, has_side_effects=True, vmem_limit_bytes=58 << 20),
        cost_estimate=pl.CostEstimate(flops=flops, bytes_accessed=20 << 20, transcendentals=0),
    )(features, w_point, w_rate_six, w_rate_twelve, w_rate_eighteen, w_pool, w_proj)
    return out.reshape(ROWS, COLS, OUT)


def solution(mesh):
    placed = (P("row", "col", None), P(), P(), P(), P(), P(), P())
    return jax.shard_map(
        functools.partial(per_device, mesh.shape["row"], mesh.shape["col"]),
        mesh=mesh, in_specs=placed, out_specs=P("row", "col", None), check_vma=False)
```

time: 350 us -> 46.3 us (0.13)
  the two profiles are of different devices: /device:TPU:1 before, /device:TPU:25 now
where the time goes in v1:
time: 46.3 us; the launch traced here: 45.8 us
  Pallas kernels  38.2 us (83%)
  local copies, waits for them, and re-layouts  7.56 us (16%)
    pallas_call x1, Pallas kernels, per_device(): pl.pallas_call(functools.partial(body, n_row, n_col), name='aspp_head', o...  38.2 us
    unnamed x1, local copies, waits for them, and re-layouts  5.65 us
    reshape x2, local copies, waits for them, and re-layouts, per_device(): return out.reshape(ROWS, COLS, OUT)  1.91 us

profile of v1, /device:TPU:25, one launch (start us, length us, event | category | flops | bytes accessed | tf_op | source)
XLA Modules:
  0.0 45.8 jit_solution(291522108655786324)
XLA Ops:
  0.0 5.6 %copy.10.x_hbm = bf16[40,20,2048]{2,1,0:T(8,128)(2,1)} copy(bf16[40,20,2048]{2,0,1:T(8,128)(2,1)} %param.7) | data formatting | bytes 6553600 | tf_op args[0]
  5.6 38.2 %aspp_head.1 = bf16[800,256]{1,0:T(8,128)(2,1)} custom-call(bf16[40,20,2048]{2,1,0:T(8,128)(2,1)} %copy.10.x_hbm, bf16[2048,128]{1,0:T(8,128)(2,1)} %wp_hbm.1, bf16[3,3,2048,128]{3,2,1,0:T(8,128)(2,1)} %w6_hbm.1, bf16[3,3,2048,128]{3,2,1,0:T(8,128)(2,1)} %w12_hbm.1, bf16[3,3,2048,128]{3,2,1,0:T(8,128)(2,1)} %w18_hbm.1, bf16[2048,128]{1,0:T(8,128)(2,1)} %wpool_hbm.1, ...), custom_call_target="tpu_custom_call" | custom-call | flops 12006195200 | bytes 20971520 | tf_op jit(solution)/shard_map/aspp_head/pallas_call | solution.py:315
  43.8 1.1 %reshape.3 = bf16[40,20,256]{2,1,0:T(8,128)(2,1)S(1)} reshape(bf16[800,256]{1,0:T(8,128)(2,1)} %aspp_head.1) | data formatting | bytes 819200 | tf_op jit(solution)/shard_map/reshape | solution.py:326
  44.9 0.8 %copy.11 = bf16[40,20,256]{2,0,1:T(8,128)(2,1)} copy(bf16[40,20,256]{2,1,0:T(8,128)(2,1)S(1)} %reshape.3) | data formatting | bytes 819200 | tf_op jit(solution)/shard_map/reshape | solution.py:326

commit v2 on v0

v2 whole, which is shorter than its diff:
```python
import functools

import jax
import jax.numpy as jnp
from jax import lax
from jax.experimental import pallas as pl
from jax.experimental.pallas import tpu as pltpu
from jax.sharding import PartitionSpec as P

MESH = pl.DeviceIdType.MESH
BF = jnp.bfloat16
F32 = jnp.float32
RATES = (18, 12, 6)
ROWS, COLS, BR, OUT = 40, 20, 128, 256
PIX = ROWS * COLS
PACK = {18: 8, 12: 4, 6: 8}
XPARTS = 5
STEPS, TAPS = 7, 4
PLANE = {d: PIX + 2 * d * ROWS for d in RATES}
BASE = {18: 0, 12: 3 * PLANE[18], 6: 3 * (PLANE[18] + PLANE[12])}
POINT = 3 * (PLANE[18] + PLANE[12] + PLANE[6])


def up16(n):
    return -(-n // 16) * 16


def take(buf, start, stop):
    low, high = start // 16 * 16, up16(stop)
    return buf[low:high].astype(F32)[start - low : stop - low]


def taps_of(step):
    if step == STEPS - 1:
        return [(18, 1, 1), (12, 1, 1), (6, 1, 1), None]
    d = RATES[step // 2]
    pairs = [(0, 2), (2, 2), (0, 0), (2, 0)] if step % 2 == 0 else [(0, 1), (2, 1), (1, 2), (1, 0)]
    return [(d, a, b) for a, b in pairs]


def places(step):
    i, odd, last = step // 2, step % 2, step // (STEPS - 1)
    s = 18 * ROWS - 6 * ROWS * i
    plane = PIX + 2 * s
    base = 3 * PLANE[18] * i - 3 * 6 * ROWS * i * (i - 1)
    even = [base, base + 2 * plane, base + 2 * s, base + 2 * plane + 2 * s]
    uneven = [base + s, base + 2 * plane + s, base + plane, base + plane + 2 * s]
    end = [BASE[d] + PLANE[d] + ROWS * d for d in RATES] + [POINT]
    return [(1 - last) * ((1 - odd) * e + odd * u) + last * z for e, u, z in zip(even, uneven, end)]


def body(
    n_row, n_col,
    x_hbm, wp_hbm, w6_hbm, w12_hbm, w18_hbm, wpool_hbm,
    joined,
    x, w, wpool, z,
    cu18, cu12, cu6, cd18, cd12, cd6, hu18, hu12, hu6, hd18, hd12, hd6,
    gcu18, gcu12, gcu6, gcd18, gcd12, gcd6, ghu18, ghu12, ghu6, ghd18, ghd12, ghd6,
    sl18, sl12, sl6, sr18, sr12, sr6, rl18, rl12, rl6, rr18, rr12, rr6,
    prow, pcol,
    xsem, wsem, wpsem, row_ss, row_rs, own_ss, own_rs, col_ss, col_rs, pr_ss, pr_rs, pc_ss, pc_rs,
):
    r = lax.axis_index("row")
    c = lax.axis_index("col")
    has_up, has_down = r > 0, r < n_row - 1
    has_left, has_right = c > 0, c < n_col - 1
    up, down = lax.rem(r + n_row - 1, n_row), lax.rem(r + 1, n_row)
    left, right = lax.rem(c + n_col - 1, n_col), lax.rem(c + 1, n_col)

    by = lambda *bufs: dict(zip(RATES, bufs))
    CU, CD, HU, HD = by(cu18, cu12, cu6), by(cd18, cd12, cd6), by(hu18, hu12, hu6), by(hd18, hd12, hd6)
    GCU, GCD = by(gcu18, gcu12, gcu6), by(gcd18, gcd12, gcd6)
    GHU, GHD = by(ghu18, ghu12, ghu6), by(ghd18, ghd12, ghd6)
    SL, SR, RL, RR = by(sl18, sl12, sl6), by(sr18, sr12, sr6), by(rl18, rl12, rl6), by(rr18, rr12, rr6)
    RATE_HBM = {18: w18_hbm, 12: w12_hbm, 6: w6_hbm}

    def start_weights(step):
        for k, tap in enumerate(taps_of(step)):
            src = wp_hbm if tap is None else RATE_HBM[tap[0]].at[tap[1], tap[2]]
            pltpu.make_async_copy(src, w.at[step, k], wsem.at[step]).start()

    start_weights(0)
    xcopies = []
    part = PIX // XPARTS
    for i in range(XPARTS):
        cp = pltpu.make_async_copy(x_hbm.at[pl.ds(part * i, part)], x.at[pl.ds(part * i, part)], xsem.at[i])
        cp.start()
        xcopies.append(cp)
    pool_weights = pltpu.make_async_copy(wpool_hbm, wpool, wpsem.at[0])

    barrier = pltpu.get_barrier_semaphore()
    for k in range(1, n_row):
        pl.semaphore_signal(barrier, inc=1, device_id=(lax.rem(r + k, n_row), c), device_id_type=MESH)
    for k in range(1, n_col):
        pl.semaphore_signal(barrier, inc=1, device_id=(r, lax.rem(c + k, n_col)), device_id_type=MESH)

    for there, bufs in ((has_up, (GCD, GHD)), (has_down, (GCU, GHU)), (has_left, (RL,)), (has_right, (RR,))):
        @pl.when(jnp.logical_not(there))
        def _(bufs=bufs):
            for buf in bufs:
                for d in RATES:
                    buf[d][...] = jnp.zeros_like(buf[d])

    @pl.loop(0, z.shape[0] // 160)
    def _(i):
        z[pl.ds(pl.multiple_of(i * 160, 160), 160)] = jnp.zeros((160, BR), F32)

    chans = x.shape[1]
    lanes = chans // BR
    acc = jnp.zeros((8, chans), F32)
    for i in range(XPARTS):
        xcopies[i].wait()

        def add(k, acc, i=i):
            at = pl.multiple_of(part * i + 16 * k, 16)
            rows = x[pl.ds(at, 16)].astype(F32)
            return acc + (rows[0:8] + rows[8:16])

        acc = lax.fori_loop(0, part // 16, add, acc)
    total = jnp.sum(acc, axis=0, keepdims=True)
    prow[0] = jnp.concatenate([total[:, BR * k : BR * k + BR] for k in range(lanes)], axis=0)
    start_weights(1)
    start_weights(2)

    def pool_row(k):
        return pltpu.make_async_remote_copy(
            src_ref=prow.at[0], dst_ref=prow.at[k], send_sem=pr_ss.at[k], recv_sem=pr_rs.at[k],
            device_id=(lax.rem(r + k, n_row), c), device_id_type=MESH)

    def pool_col(k):
        return pltpu.make_async_remote_copy(
            src_ref=pcol.at[0], dst_ref=pcol.at[k], send_sem=pc_ss.at[k], recv_sem=pc_rs.at[k],
            device_id=(r, lax.rem(c + k, n_col)), device_id_type=MESH)

    def corner_copy(d, way):
        n = 2 * RATES.index(d) + way
        src, dst, to = ((CU[d], GCU[d], up), (CD[d], GCD[d], down))[way]
        return pltpu.make_async_remote_copy(
            src_ref=src, dst_ref=dst, send_sem=row_ss.at[n], recv_sem=row_rs.at[n],
            device_id=(to, c), device_id_type=MESH)

    def own_copy(d, way):
        n = 2 * RATES.index(d) + way
        src, dst, to = ((HU[d], GHU[d], up), (HD[d], GHD[d], down))[way]
        return pltpu.make_async_remote_copy(
            src_ref=src, dst_ref=dst, send_sem=own_ss.at[n], recv_sem=own_rs.at[n],
            device_id=(to, c), device_id_type=MESH)

    def col_copy(d, way):
        n = 2 * RATES.index(d) + way
        src, dst, to = ((SL[d], RR[d], left), (SR[d], RL[d], right))[way]
        return pltpu.make_async_remote_copy(
            src_ref=src, dst_ref=dst, send_sem=col_ss.at[n], recv_sem=col_rs.at[n],
            device_id=(r, to), device_id_type=MESH)

    def start(copy, d, first, second):
        @pl.when(first)
        def _():
            copy(d, 0).start()

        @pl.when(second)
        def _():
            copy(d, 1).start()

    def arrive(copy, d, first, second):
        @pl.when(first)
        def _():
            copy(d, 0).wait_recv()

        @pl.when(second)
        def _():
            copy(d, 1).wait_recv()

    def pack(d, columns, to_up, to_down):
        g = PACK[d]
        for k in range(0, len(columns), g):
            some = columns[k : k + g]
            gap = [jnp.zeros((up16(len(some) * d) - len(some) * d, BR), F32)] if len(some) * d % 16 else []
            at2 = BASE[d] + 2 * PLANE[d]
            at0 = BASE[d]
            rows = slice(k * d, k * d + up16(len(some) * d))
            to_up[rows] = jnp.concatenate(
                [z[at2 + ROWS * j : at2 + ROWS * (j + 1)][0:d] for j in some] + gap, axis=0).astype(BF)
            to_down[rows] = jnp.concatenate(
                [z[at0 + ROWS * j : at0 + ROWS * (j + 1)][ROWS - d : ROWS] for j in some] + gap, axis=0).astype(BF)

    def corners_out(d):
        pack(d, list(range(d)) + list(range(d + COLS, COLS + 2 * d)), CU[d], CD[d])
        start(corner_copy, d, has_up, has_down)

    def own_out(d):
        pack(d, list(range(d, d + COLS)), HU[d], HD[d])
        start(own_copy, d, has_up, has_down)

    def summed(d, first, count, got_u, got_d, k):
        z0, z1, z2 = (z[BASE[d] + a * PLANE[d] + ROWS * first : BASE[d] + a * PLANE[d] + ROWS * (first + count)]
                      for a in range(3))
        got_u = take(got_u, k * d, (k + count) * d)
        got_d = take(got_d, k * d, (k + count) * d)
        above, below = [], []
        for k in range(count):
            above += [got_d[k * d : (k + 1) * d], z0[ROWS * k : ROWS * (k + 1) - d]]
            below += [z2[ROWS * k + d : ROWS * (k + 1)], got_u[k * d : (k + 1) * d]]
        return z1 + jnp.concatenate(above, axis=0) + jnp.concatenate(below, axis=0)

    def cols_out(d):
        arrive(corner_copy, d, has_down, has_up)
        for k in range(0, d, 6):
            rows = slice(ROWS * k, ROWS * (k + 6))
            SL[d][rows] = summed(d, k, 6, GCU[d], GCD[d], k).astype(BF)
            SR[d][rows] = summed(d, COLS + d + k, 6, GCU[d], GCD[d], d + k).astype(BF)
        start(col_copy, d, has_left, has_right)

    def own_in(d):
        arrive(own_copy, d, has_down, has_up)
        for k in range(0, COLS, 4):
            at = BASE[d] + PLANE[d] + ROWS * (d + k)
            z[at : at + 4 * ROWS] = summed(d, d + k, 4, GHU[d], GHD[d], k)

    def pool_first():
        for k in range(1, n_row):
            pool_row(k).start()

    def pool_second():
        for k in range(1, n_row):
            pool_row(k).wait_recv()
        acc = prow[0]
        for k in range(1, n_row):
            acc = acc + prow[k]
        pcol[0] = acc
        for k in range(1, n_col):
            pool_col(k).start()

    def pool_third():
        for k in range(1, n_col):
            pool_col(k).wait_recv()
        acc = pcol[0]
        for k in range(1, n_col):
            acc = acc + pcol[k]
        pooled = (acc / (PIX * n_row * n_col)).astype(BF).astype(F32)
        pool_weights.wait()
        side = jnp.transpose(pooled, (1, 0))
        parts = jnp.zeros((8, BR), F32)
        for k in range(lanes):
            prod = side[:, k : k + 1] * wpool[BR * k : BR * k + BR].astype(F32)
            parts = parts + jnp.sum(prod.reshape(BR // 8, 8, BR), axis=0)
        branch = jnp.maximum(jnp.sum(parts, axis=0, keepdims=True), 0.0)
        joined[:, 4 * BR : 5 * BR] = jnp.broadcast_to(branch, (PIX, BR)).astype(BF)

    def after(step):
        if step == 0:
            pl.semaphore_wait(barrier, n_row + n_col - 2)
            corners_out(18)
            pool_first()
            start_weights(3)
        elif step == 1:
            start_weights(4)
            own_out(18)
        elif step == 2:
            corners_out(12)
            start_weights(5)
            pool_second()
        elif step == 3:
            start_weights(6)
            pool_weights.start()
            cols_out(18)
            own_out(12)
        elif step == 4:
            corners_out(6)
            cols_out(12)
        elif step == 5:
            own_out(6)
            cols_out(6)
            pool_third()

    @pl.loop(0, STEPS)
    def _(step):
        pltpu.make_async_copy(w.at[step], w.at[step], wsem.at[step]).wait()
        taps = jnp.concatenate([w[step, k] for k in range(TAPS)], axis=1)
        y = jnp.dot(x[...], taps, preferred_element_type=F32)
        for k, at in enumerate(places(step)):
            rows = pl.ds(pl.multiple_of(at, 8), PIX)
            z[rows] += y[:, BR * k : BR * k + BR]
        for s in range(STEPS - 1):
            @pl.when(step == s)
            def _(s=s):
                after(s)

    joined[:, 0:BR] = jnp.maximum(z[POINT : POINT + PIX], 0.0).astype(BF)
    for d in RATES:
        own_in(d)
    for n, d in ((3, 18), (2, 12), (1, 6)):
        arrive(col_copy, d, has_right, has_left)
        at = BASE[d] + PLANE[d] + ROWS * d
        for k in range(0, COLS, 2):
            whole = z[at + ROWS * k : at + ROWS * (k + 2)]
            if k < d:
                whole = whole + RL[d][ROWS * k : ROWS * (k + 2)].astype(F32)
            if k >= COLS - d:
                j = k - (COLS - d)
                whole = whole + RR[d][ROWS * j : ROWS * (j + 2)].astype(F32)
            joined[ROWS * k : ROWS * (k + 2), BR * n : BR * (n + 1)] = jnp.maximum(whole, 0.0).astype(BF)

    for k in range(1, n_row):
        pool_row(k).wait_send()
    for k in range(1, n_col):
        pool_col(k).wait_send()
    for d in RATES:
        for there, copy in (
            (has_up, corner_copy(d, 0)), (has_down, corner_copy(d, 1)), (has_up, own_copy(d, 0)),
            (has_down, own_copy(d, 1)), (has_left, col_copy(d, 0)), (has_right, col_copy(d, 1)),
        ):
            @pl.when(there)
            def _(copy=copy):
                copy.wait_send()


def per_device(n_row, n_col, features, w_point, w_rate_six, w_rate_twelve, w_rate_eighteen, w_pool, w_proj):
    chans = features.shape[2]
    lanes = chans // BR
    vm = pltpu.VMEM
    dma = pltpu.SemaphoreType.DMA
    scratch = [vm((PIX, chans), BF), vm((STEPS, TAPS, chans, BR), BF), vm((chans, BR), BF), vm((POINT + PIX, BR), F32)]
    for _ in range(2):
        for _ in range(2):
            scratch += [vm((up16(2 * d * d), BR), BF) for d in RATES]
        for _ in range(2):
            scratch += [vm((up16(COLS * d), BR), BF) for d in RATES]
    for _ in range(4):
        scratch += [vm((ROWS * d, BR), BF) for d in RATES]
    scratch += [vm((n_row, lanes, BR), F32), vm((n_col, lanes, BR), F32)]
    scratch += [dma((XPARTS,)), dma((STEPS,)), dma((1,))] + [dma((6,))] * 6
    scratch += [dma((n_row,)), dma((n_row,)), dma((n_col,)), dma((n_col,))]
    pixels = jnp.transpose(features, (1, 0, 2)).reshape(PIX, chans)
    joined = pl.pallas_call(
        functools.partial(body, n_row, n_col),
        name="aspp_branches",
        out_shape=jax.ShapeDtypeStruct((PIX, 5 * BR), BF),
        in_specs=[pl.BlockSpec(memory_space=pl.ANY)] * 6,
        out_specs=pl.BlockSpec(memory_space=pltpu.VMEM),
        scratch_shapes=scratch,
        compiler_params=pltpu.CompilerParams(
            collective_id=0, has_side_effects=True, vmem_limit_bytes=58 << 20),
        cost_estimate=pl.CostEstimate(
            flops=2 * PIX * chans * BR * 28, bytes_accessed=20 << 20, transcendentals=0),
    )(pixels, w_point, w_rate_six, w_rate_twelve, w_rate_eighteen, w_pool)
    mixed = jnp.dot(joined, w_proj, preferred_element_type=F32)
    out = jnp.maximum(mixed, 0.0).astype(BF)
    return jnp.transpose(out.reshape(COLS, ROWS, OUT), (1, 0, 2))


def solution(mesh):
    placed = (P("row", "col", None), P(), P(), P(), P(), P(), P())
    return jax.shard_map(
        functools.partial(per_device, mesh.shape["row"], mesh.shape["col"]),
        mesh=mesh, in_specs=placed, out_specs=P("row", "col", None), check_vma=False)
```

time: 350 us -> 34.5 us (0.10)
  the two profiles are of different devices: /device:TPU:1 before, /device:TPU:25 now
where the time goes in v2:
time: 34.5 us; the launch traced here: 34.4 us
  Pallas kernels  31.9 us (92%)
  matrix products  2.46 us (7%)
    pallas_call x1, Pallas kernels, per_device(): pl.pallas_call(functools.partial(body, n_row, n_col), name='aspp_branches...  31.9 us
    dot_general x1, matrix products, per_device(): mixed = jnp.dot(joined, w_proj, preferred_element_type=F32)  2.46 us

profile of v2, /device:TPU:25, one launch (start us, length us, event | category | flops | bytes accessed | tf_op | source)
XLA Modules:
  0.0 34.4 jit_solution(5007357950991081224)
XLA Ops:
  0.0 0.0 copy-start
  0.0 31.9 %aspp_branches.1 = bf16[800,640]{1,0:T(8,128)(2,1)} custom-call(bf16[800,2048]{1,0:T(8,128)(2,1)} %bitcast.8, bf16[2048,128]{1,0:T(8,128)(2,1)} %wp_hbm.1, bf16[3,3,2048,128]{3,2,1,0:T(8,128)(2,1)} %w6_hbm.1, bf16[3,3,2048,128]{3,2,1,0:T(8,128)(2,1)} %w12_hbm.1, bf16[3,3,2048,128]{3,2,1,0:T(8,128)(2,1)} %w18_hbm.1, bf16[2048,128]{1,0:T(8,128)(2,1)} %wpool_hbm.1), custom_call_target="tpu_custom_call" | custom-call | flops 11744051200 | bytes 20971520 | tf_op jit(solution)/shard_map/aspp_branches/pallas_call | solution.py:335
  31.9 0.0 copy-done
  31.9 2.5 %fusion = bf16[800,256]{1,0:T(8,128)(2,1)} fusion(bf16[800,640]{1,0:T(8,128)(2,1)} %aspp_branches.1, bf16[640,256]{1,0:T(8,128)(2,1)S(1)} %copy-done), kind=kOutput, calls=%fused_computation.1 | convolution fusion | flops 262553600 | bytes 1761280 | tf_op jit(solution)/shard_map/dot_general | solution.py:347
Async XLA Ops:
  0.0 31.9 %copy-start = (bf16[640,256]{1,0:T(8,128)(2,1)S(1)}, bf16[640,256]{1,0:T(8,128)(2,1)}, u32[]{:S(2)}) copy-start(bf16[640,256]{1,0:T(8,128)(2,1)} %param.13) | copy-start | bytes 983044

commit v3 on v2

v3 whole, which is shorter than its diff:
```python
import functools

import jax
import jax.numpy as jnp
from jax import lax
from jax.experimental import pallas as pl
from jax.experimental.pallas import tpu as pltpu
from jax.sharding import PartitionSpec as P

MESH = pl.DeviceIdType.MESH
BF = jnp.bfloat16
F32 = jnp.float32
RATES = (18, 12, 6)
ROWS, COLS, BR, OUT = 40, 20, 128, 256
PIX = ROWS * COLS
PACK = {18: 8, 12: 4, 6: 8}
XPARTS = 5
STEPS, TAPS = 7, 4
PLANE = {d: COLS + 2 * d for d in RATES}
BASE = {18: 0, 12: 3 * PLANE[18], 6: 3 * (PLANE[18] + PLANE[12])}
POINT = 3 * (PLANE[18] + PLANE[12] + PLANE[6])


def up16(n):
    return -(-n // 16) * 16


def up8(n):
    return -(-n // 8) * 8


def take(buf, start, stop):
    low, high = start // 16 * 16, up16(stop)
    return buf[low:high].astype(F32)[start - low : stop - low]


def taps_of(step):
    if step == STEPS - 1:
        return [(18, 1, 1), (12, 1, 1), (6, 1, 1), None]
    d = RATES[step // 2]
    pairs = [(0, 2), (2, 2), (0, 0), (2, 0)] if step % 2 == 0 else [(0, 1), (2, 1), (1, 2), (1, 0)]
    return [(d, a, b) for a, b in pairs]


def body(
    n_row, n_col,
    x_hbm, wp_hbm, w6_hbm, w12_hbm, w18_hbm, wpool_hbm, wproj_hbm,
    out_ref,
    x, w, wpool, wproj, z, joined,
    cu18, cu12, cu6, cd18, cd12, cd6, gcu18, gcu12, gcu6, gcd18, gcd12, gcd6,
    hu18, hu12, hu6, hd18, hd12, hd6, ghu18, ghu12, ghu6, ghd18, ghd12, ghd6,
    so18, so12, so6, si18, si12, si6, ro18, ro12, ro6, ri18, ri12, ri6,
    iu18, iu12, iu6, id18, id12, id6,
    prow, pcol,
    xsem, wsem, wpsem, row_ss, row_rs, own_ss, own_rs, col_ss, col_rs, in_ss, in_rs, pr_ss, pr_rs, pc_ss, pc_rs,
):
    r = lax.axis_index("row")
    c = lax.axis_index("col")
    core = lax.rem(c, 2)
    has_up, has_down = r > 0, r < n_row - 1
    has_outer = jnp.logical_and(c > 0, c < n_col - 1)
    up, down = lax.rem(r + n_row - 1, n_row), lax.rem(r + 1, n_row)
    outer, inner = lax.rem(c + n_col - 1 + 2 * core, n_col), c + 1 - 2 * core

    by = lambda *bufs: dict(zip(RATES, bufs))
    CU, CD, GCU, GCD = by(cu18, cu12, cu6), by(cd18, cd12, cd6), by(gcu18, gcu12, gcu6), by(gcd18, gcd12, gcd6)
    HU, HD, GHU, GHD = by(hu18, hu12, hu6), by(hd18, hd12, hd6), by(ghu18, ghu12, ghu6), by(ghd18, ghd12, ghd6)
    SO, SI, RO, RI = by(so18, so12, so6), by(si18, si12, si6), by(ro18, ro12, ro6), by(ri18, ri12, ri6)
    IU, ID = by(iu18, iu12, iu6), by(id18, id12, id6)
    RATE_HBM = {18: w18_hbm, 12: w12_hbm, 6: w6_hbm}

    def start_weights(step):
        for k, tap in enumerate(taps_of(step)):
            src = wp_hbm if tap is None else RATE_HBM[tap[0]].at[tap[1], tap[2]]
            pltpu.make_async_copy(src, w.at[step, k], wsem.at[step]).start()

    start_weights(0)
    xcopies = []
    part = PIX // XPARTS
    for i in range(XPARTS):
        cp = pltpu.make_async_copy(x_hbm.at[pl.ds(part * i, part)], x.at[pl.ds(part * i, part)], xsem.at[i])
        cp.start()
        xcopies.append(cp)
    late = [pltpu.make_async_copy(wpool_hbm, wpool, wpsem.at[0]), pltpu.make_async_copy(wproj_hbm, wproj, wpsem.at[1])]

    barrier = pltpu.get_barrier_semaphore()
    for k in range(1, n_row):
        pl.semaphore_signal(barrier, inc=1, device_id=(lax.rem(r + k, n_row), c), device_id_type=MESH)
    for k in range(1, n_col):
        pl.semaphore_signal(barrier, inc=1, device_id=(r, lax.rem(c + k, n_col)), device_id_type=MESH)

    for there, bufs in ((has_up, (GCD, GHD)), (has_down, (GCU, GHU)), (has_outer, (RO,))):
        @pl.when(jnp.logical_not(there))
        def _(bufs=bufs):
            for buf in bufs:
                for d in RATES:
                    buf[d][...] = jnp.zeros_like(buf[d])

    chans = x.shape[1]
    lanes = chans // BR
    acc = jnp.zeros((8, chans), F32)
    for i in range(XPARTS):
        xcopies[i].wait()

        def add(k, acc, i=i):
            at = pl.multiple_of(part * i + 16 * k, 16)
            rows = x[pl.ds(at, 16)].astype(F32)
            return acc + (rows[0:8] + rows[8:16])

        acc = lax.fori_loop(0, part // 16, add, acc)
    total = jnp.sum(acc, axis=0, keepdims=True)
    prow[0] = jnp.concatenate([total[:, BR * k : BR * k + BR] for k in range(lanes)], axis=0)
    start_weights(1)
    start_weights(2)

    def remote(src, dst, sems, n, to):
        return pltpu.make_async_remote_copy(
            src_ref=src, dst_ref=dst, send_sem=sems[0].at[n], recv_sem=sems[1].at[n],
            device_id=to, device_id_type=MESH)

    def pool_row(k):
        return remote(prow.at[0], prow.at[k], (pr_ss, pr_rs), k, (lax.rem(r + k, n_row), c))

    def pool_col(k):
        return remote(pcol.at[0], pcol.at[k], (pc_ss, pc_rs), k, (r, lax.rem(c + k, n_col)))

    def corner_copies(d):
        n = 2 * RATES.index(d)
        return (lambda: remote(CU[d], GCU[d], (row_ss, row_rs), n, (up, c)),
                lambda: remote(CD[d], GCD[d], (row_ss, row_rs), n + 1, (down, c)))

    def own_copies(d):
        n = 2 * RATES.index(d)
        return (lambda: remote(HU[d], GHU[d], (own_ss, own_rs), n, (up, c)),
                lambda: remote(HD[d], GHD[d], (own_ss, own_rs), n + 1, (down, c)))

    def side_copies(d):
        n = 2 * RATES.index(d)
        return (lambda: remote(SO[d], RO[d], (col_ss, col_rs), n, (r, outer)),
                lambda: remote(SI[d], RI[d], (col_ss, col_rs), n + 1, (r, inner)))

    def inner_copies(d):
        n = 2 * RATES.index(d)
        high = up8(d)
        at = (1 - core) * (COLS + d)
        src_u = z.at[pl.ds(BASE[d] + 2 * PLANE[d] + at, d), pl.ds(0, high)]
        src_d = z.at[pl.ds(BASE[d] + at, d), pl.ds(ROWS - high, high)]
        return (lambda: remote(src_u, IU[d], (in_ss, in_rs), n, (r, inner)),
                lambda: remote(src_d, ID[d], (in_ss, in_rs), n + 1, (r, inner)))

    def start_rows(copies):
        @pl.when(has_up)
        def _():
            copies[0]().start()

        @pl.when(has_down)
        def _():
            copies[1]().start()

    def arrive_rows(copies):
        @pl.when(has_down)
        def _():
            copies[0]().wait_recv()

        @pl.when(has_up)
        def _():
            copies[1]().wait_recv()

    def pack(d, at, count, to_up, to_down):
        g = PACK[d]
        for k in range(0, count, g):
            n = min(g, count - k)
            gap = [jnp.zeros((up16(n * d) - n * d, BR), F32)] if n * d % 16 else []
            rows = slice(k * d, k * d + up16(n * d))
            tops = [z[BASE[d] + 2 * PLANE[d] + at + k + j][0:d] for j in range(n)]
            ends = [z[BASE[d] + at + k + j][ROWS - d : ROWS] for j in range(n)]
            to_up[rows] = jnp.concatenate(tops + gap, axis=0).astype(BF)
            to_down[rows] = jnp.concatenate(ends + gap, axis=0).astype(BF)

    def summed(d, at, count, got=None, k=0):
        if got is None:
            got_u = got_d = jnp.zeros((count * d, BR), F32)
        else:
            got_u, got_d = (take(buf[d], k * d, (k + count) * d) for buf in got)
        above, below, same = [], [], []
        for j in range(count):
            z0, z1, z2 = (z[BASE[d] + a * PLANE[d] + at + j] for a in range(3))
            above += [got_d[j * d : (j + 1) * d], z0[0 : ROWS - d]]
            below += [z2[d:ROWS], got_u[j * d : (j + 1) * d]]
            same.append(z1)
        return sum(jnp.concatenate(parts, axis=0) for parts in (same, above, below))

    def corners_out(d):
        pack(d, core * (COLS + d), d, CU[d], CD[d])
        start_rows(corner_copies(d))
        for copy in inner_copies(d):
            copy().start()

    def own_pack(d):
        for copy in inner_copies(d):
            copy().wait_recv()
        high = up8(d)
        at = d + (1 - core) * (COLS - d)
        row = lax.broadcasted_iota(jnp.int32, (d, high, BR), 1)
        z[pl.ds(BASE[d] + 2 * PLANE[d] + at, d), 0:high] += jnp.where(row < d, IU[d][...], 0.0)
        z[pl.ds(BASE[d] + at, d), ROWS - high : ROWS] += jnp.where(row >= high - d, ID[d][...], 0.0)
        pack(d, d, COLS, HU[d], HD[d])

    def inner_side(d):
        at = (1 - core) * (COLS + d)
        for k in range(0, d, 6):
            SI[d][ROWS * k : ROWS * (k + 6)] = summed(d, at + k, 6).astype(BF)
        side_copies(d)[1]().start()

    def outer_side(d):
        arrive_rows(corner_copies(d))
        at = core * (COLS + d)
        for k in range(0, d, 6):
            SO[d][ROWS * k : ROWS * (k + 6)] = summed(d, at + k, 6, (GCU, GCD), k).astype(BF)

        @pl.when(has_outer)
        def _():
            side_copies(d)[0]().start()

    def own_in(d):
        arrive_rows(own_copies(d))
        for k in range(0, COLS, 4):
            at = BASE[d] + PLANE[d] + d + k
            z[at : at + 4] = summed(d, d + k, 4, (GHU, GHD), k).reshape(4, ROWS, BR)

    def pool_first():
        for k in range(1, n_row):
            pool_row(k).start()

    def pool_second():
        for k in range(1, n_row):
            pool_row(k).wait_recv()
        acc = prow[0]
        for k in range(1, n_row):
            acc = acc + prow[k]
        pcol[0] = acc
        for k in range(1, n_col):
            pool_col(k).start()

    def pool_third():
        for k in range(1, n_col):
            pool_col(k).wait_recv()
        acc = pcol[0]
        for k in range(1, n_col):
            acc = acc + pcol[k]
        pooled = (acc / (PIX * n_row * n_col)).astype(BF).astype(F32)
        side = jnp.transpose(pooled, (1, 0))
        parts = jnp.zeros((8, BR), F32)
        for k in range(lanes):
            prod = side[:, k : k + 1] * wpool[BR * k : BR * k + BR].astype(F32)
            parts = parts + jnp.sum(prod.reshape(BR // 8, 8, BR), axis=0)
        branch = jnp.maximum(jnp.sum(parts, axis=0, keepdims=True), 0.0)
        branch = jnp.broadcast_to(branch, (16, BR)).astype(BF)
        return jnp.dot(branch, wproj[4 * BR : 5 * BR], preferred_element_type=F32)[0:1]

    filled = set()

    def put(at, y):
        y = y.reshape(COLS, ROWS, BR)
        k = 0
        while k < COLS:
            old = at + k in filled
            n = 1
            while k + n < COLS and (at + k + n in filled) == old:
                n += 1
            if old:
                z[at + k : at + k + n] += y[k : k + n]
            else:
                z[at + k : at + k + n] = y[k : k + n]
            k += n
        filled.update(range(at, at + COLS))

    def multiply(step):
        pltpu.make_async_copy(w.at[step], w.at[step], wsem.at[step]).wait()
        if step + 3 < STEPS:
            start_weights(step + 3)
        if step == 3:
            for copy in late:
                copy.start()
        taps = jnp.concatenate([w[step, k] for k in range(TAPS)], axis=1)
        half = PIX // 2
        y = jnp.concatenate(
            [jnp.dot(x[at : at + half], taps, preferred_element_type=F32) for at in (0, half)], axis=0)
        for k, tap in enumerate(taps_of(step)):
            at = POINT
            if tap is not None:
                d, a, b = tap
                at = BASE[d] + a * PLANE[d] + (2 - b) * d
            put(at, y[:, BR * k : BR * k + BR])

    hole = BASE[18] + PLANE[18] + COLS
    z[hole : hole + 36 - COLS] = jnp.zeros((36 - COLS, ROWS, BR), F32)
    filled.update(range(hole, hole + 36 - COLS))

    multiply(0)
    pl.semaphore_wait(barrier, n_row + n_col - 2)
    corners_out(18)
    pool_first()
    multiply(1)
    own_pack(18)
    inner_side(18)
    multiply(2)
    corners_out(12)
    start_rows(own_copies(18))
    outer_side(18)
    pool_second()
    multiply(3)
    own_pack(12)
    inner_side(12)
    start_rows(own_copies(12))
    multiply(4)
    corners_out(6)
    outer_side(12)
    multiply(5)
    own_pack(6)
    inner_side(6)
    outer_side(6)
    start_rows(own_copies(6))
    multiply(6)
    for copy in late:
        copy.wait()
    for d in RATES:
        own_in(d)
    pool_part = pool_third()
    joined[:, 0:BR] = jnp.maximum(z[POINT : POINT + COLS], 0.0).reshape(PIX, BR).astype(BF)

    for n, d in ((3, 18), (2, 12), (1, 6)):
        side_copies(d)[1]().wait_recv()

        @pl.when(has_outer)
        def _(d=d):
            side_copies(d)[0]().wait_recv()

        at = BASE[d] + PLANE[d] + d
        for buf, side in ((RO[d], core), (RI[d], 1 - core)):
            z[pl.ds(at + side * (COLS - d), d)] += buf[...].astype(F32).reshape(d, ROWS, BR)
        joined[:, BR * n : BR * (n + 1)] = jnp.maximum(z[at : at + COLS], 0.0).reshape(PIX, BR).astype(BF)

    for at in (0, PIX // 2):
        rows = slice(at, at + PIX // 2)
        mixed = jnp.dot(joined[rows], wproj[0 : 4 * BR], preferred_element_type=F32)
        out_ref[rows] = jnp.maximum(mixed + pool_part, 0.0).astype(BF)

    for k in range(1, n_row):
        pool_row(k).wait_send()
    for k in range(1, n_col):
        pool_col(k).wait_send()
    for d in RATES:
        inner_copies(d)[0]().wait_send()
        inner_copies(d)[1]().wait_send()
        side_copies(d)[1]().wait_send()
        for there, copy in (
            (has_up, corner_copies(d)[0]), (has_down, corner_copies(d)[1]),
            (has_up, own_copies(d)[0]), (has_down, own_copies(d)[1]), (has_outer, side_copies(d)[0]),
        ):
            @pl.when(there)
            def _(copy=copy):
                copy().wait_send()


def per_device(n_row, n_col, features, w_point, w_rate_six, w_rate_twelve, w_rate_eighteen, w_pool, w_proj):
    chans = features.shape[2]
    lanes = chans // BR
    vm = pltpu.VMEM
    dma = pltpu.SemaphoreType.DMA
    scratch = [vm((PIX, chans), BF), vm((STEPS, TAPS, chans, BR), BF), vm((chans, BR), BF), vm((5 * BR, OUT), BF)]
    scratch += [vm((POINT + COLS, ROWS, BR), F32), vm((PIX, 4 * BR), BF)]
    for size in (lambda d: up16(d * d), lambda d: up16(COLS * d), lambda d: ROWS * d):
        for _ in range(4):
            scratch += [vm((size(d), BR), BF) for d in RATES]
    for _ in range(2):
        scratch += [vm((d, up8(d), BR), F32) for d in RATES]
    scratch += [vm((n_row, lanes, BR), F32), vm((n_col, lanes, BR), F32)]
    scratch += [dma((XPARTS,)), dma((STEPS,)), dma((2,))] + [dma((6,))] * 8
    scratch += [dma((n_row,)), dma((n_row,)), dma((n_col,)), dma((n_col,))]
    pixels = jnp.transpose(features, (1, 0, 2)).reshape(PIX, chans)
    out = pl.pallas_call(
        functools.partial(body, n_row, n_col),
        name="aspp_branches",
        out_shape=jax.ShapeDtypeStruct((PIX, OUT), BF),
        in_specs=[pl.BlockSpec(memory_space=pltpu.HBM)] * 7,
        out_specs=pl.BlockSpec(memory_space=pltpu.VMEM),
        scratch_shapes=scratch,
        compiler_params=pltpu.CompilerParams(
            collective_id=0, has_side_effects=True, vmem_limit_bytes=48 << 20),
        cost_estimate=pl.CostEstimate(
            flops=2 * PIX * chans * BR * 28, bytes_accessed=20 << 20, transcendentals=0),
    )(*[pltpu.with_memory_space_constraint(a, pltpu.HBM) for a in (
        pixels, w_point, w_rate_six, w_rate_twelve, w_rate_eighteen, w_pool, w_proj)])
    return jnp.transpose(out.reshape(COLS, ROWS, OUT), (1, 0, 2))


def solution(mesh):
    placed = (P("row", "col", None), P(), P(), P(), P(), P(), P())
    return jax.shard_map(
        functools.partial(per_device, mesh.shape["row"], mesh.shape["col"]),
        mesh=mesh, in_specs=placed, out_specs=P("row", "col", None), check_vma=False)
```

time: 34.5 us -> 29.2 us (0.85)
  Pallas kernels: 31.9 us -> 28.3 us
  matrix products: 2.46 us -> 0 us
  local copies, waits for them, and re-layouts: 0.01 us -> 0.75 us
    pallas_call x1, Pallas kernels: 31.9 us -> 28.3 us  [per_device(): pl.pallas_call(functools.partial(body, n_row, n_col), name='aspp_branches...]
    dot_general x1 -> x0, matrix products: 2.46 us -> none  [per_device(): mixed = jnp.dot(joined, w_proj, preferred_element_type=F32)]
    unnamed x2 -> x1, local copies, waits for them, and re-layouts: 0.01 us -> 0.75 us
where the time goes in v3:
time: 29.2 us; the launch traced here: 29 us
  Pallas kernels  28.3 us (97%)
  local copies, waits for them, and re-layouts  0.75 us (3%)
    pallas_call x1, Pallas kernels, per_device(): pl.pallas_call(functools.partial(body, n_row, n_col), name='aspp_branches...  28.3 us
    unnamed x1, local copies, waits for them, and re-layouts  0.75 us

profile of v3, /device:TPU:25, one launch (start us, length us, event | category | flops | bytes accessed | tf_op | source)
XLA Modules:
  0.0 29.0 jit_solution(406975133561267422)
XLA Ops:
  0.0 28.3 %aspp_branches.1 = bf16[800,256]{1,0:T(8,128)(2,1)S(1)} custom-call(bf16[800,2048]{1,0:T(8,128)(2,1)} %bitcast.7, bf16[2048,128]{1,0:T(8,128)(2,1)} %wp_hbm.1, bf16[3,3,2048,128]{3,2,1,0:T(8,128)(2,1)} %w6_hbm.1, bf16[3,3,2048,128]{3,2,1,0:T(8,128)(2,1)} %w12_hbm.1, bf16[3,3,2048,128]{3,2,1,0:T(8,128)(2,1)} %w18_hbm.1, bf16[2048,128]{1,0:T(8,128)(2,1)} %wpool_hbm.1, ...), custom_call_target="tpu_custom_call" | custom-call | flops 11744051200 | bytes 20971520 | tf_op jit(solution)/shard_map/aspp_branches/pallas_call | solution.py:382
  28.3 0.8 %copy.9 = bf16[40,20,256]{2,0,1:T(8,128)(2,1)} copy(bf16[40,20,256]{2,0,1:T(8,128)(2,1)S(1)} %bitcast.6) | data formatting | bytes 819200

commit v4 on v3

--- a/solution.py
+++ b/solution.py
@@ -14,7 +14,7 @@
 ROWS, COLS, BR, OUT = 40, 20, 128, 256
 PIX = ROWS * COLS
 PACK = {18: 8, 12: 4, 6: 8}
-XPARTS = 5
+XPARTS = 2
 STEPS, TAPS = 7, 4
 PLANE = {d: COLS + 2 * d for d in RATES}
 BASE = {18: 0, 12: 3 * PLANE[18], 6: 3 * (PLANE[18] + PLANE[12])}
@@ -34,12 +34,15 @@
     return buf[low:high].astype(F32)[start - low : stop - low]
 
 
-def taps_of(step):
-    if step == STEPS - 1:
-        return [(18, 1, 1), (12, 1, 1), (6, 1, 1), None]
-    d = RATES[step // 2]
-    pairs = [(0, 2), (2, 2), (0, 0), (2, 0)] if step % 2 == 0 else [(0, 1), (2, 1), (1, 2), (1, 0)]
-    return [(d, a, b) for a, b in pairs]
+ORDER = (
+    ((18, 0, 2), (18, 2, 2), (18, 0, 0), (18, 2, 0)),
+    ((18, 0, 1), (18, 2, 1), (12, 0, 2), (12, 2, 2)),
+    ((18, 1, 2), (18, 1, 0), (12, 0, 0), (12, 2, 0)),
+    ((6, 0, 2), (6, 2, 2), (6, 0, 0), (6, 2, 0)),
+    ((12, 0, 1), (12, 2, 1), (12, 1, 2), (12, 1, 0)),
+    ((6, 0, 1), (6, 2, 1), (6, 1, 2), (6, 1, 0)),
+    ((18, 1, 1), (12, 1, 1), (6, 1, 1), None),
+)
 
 
 def body(
@@ -51,8 +54,8 @@
     hu18, hu12, hu6, hd18, hd12, hd6, ghu18, ghu12, ghu6, ghd18, ghd12, ghd6,
     so18, so12, so6, si18, si12, si6, ro18, ro12, ro6, ri18, ri12, ri6,
     iu18, iu12, iu6, id18, id12, id6,
-    prow, pcol,
-    xsem, wsem, wpsem, row_ss, row_rs, own_ss, own_rs, col_ss, col_rs, in_ss, in_rs, pr_ss, pr_rs, pc_ss, pc_rs,
+    shares, got_shares, sums, products,
+    xsem, wsem, wpsem, row_ss, row_rs, own_ss, own_rs, col_ss, col_rs, in_ss, in_rs, ps_ss, ps_rs, pc_ss, pc_rs, pp_ss, pp_rs,
 ):
     r = lax.axis_index("row")
     c = lax.axis_index("col")
@@ -70,7 +73,7 @@
     RATE_HBM = {18: w18_hbm, 12: w12_hbm, 6: w6_hbm}
 
     def start_weights(step):
-        for k, tap in enumerate(taps_of(step)):
+        for k, tap in enumerate(ORDER[step]):
             src = wp_hbm if tap is None else RATE_HBM[tap[0]].at[tap[1], tap[2]]
             pltpu.make_async_copy(src, w.at[step, k], wsem.at[step]).start()
 
@@ -98,31 +101,22 @@
 
     chans = x.shape[1]
     lanes = chans // BR
-    acc = jnp.zeros((8, chans), F32)
-    for i in range(XPARTS):
-        xcopies[i].wait()
-
-        def add(k, acc, i=i):
-            at = pl.multiple_of(part * i + 16 * k, 16)
-            rows = x[pl.ds(at, 16)].astype(F32)
-            return acc + (rows[0:8] + rows[8:16])
-
-        acc = lax.fori_loop(0, part // 16, add, acc)
-    total = jnp.sum(acc, axis=0, keepdims=True)
-    prow[0] = jnp.concatenate([total[:, BR * k : BR * k + BR] for k in range(lanes)], axis=0)
-    start_weights(1)
-    start_weights(2)
+    share = chans // n_row
 
     def remote(src, dst, sems, n, to):
         return pltpu.make_async_remote_copy(
             src_ref=src, dst_ref=dst, send_sem=sems[0].at[n], recv_sem=sems[1].at[n],
             device_id=to, device_id_type=MESH)
 
-    def pool_row(k):
-        return remote(prow.at[0], prow.at[k], (pr_ss, pr_rs), k, (lax.rem(r + k, n_row), c))
-
-    def pool_col(k):
-        return remote(pcol.at[0], pcol.at[k], (pc_ss, pc_rs), k, (r, lax.rem(c + k, n_col)))
+    def share_copy(k):
+        to = lax.rem(r + k, n_row)
+        return remote(shares.at[to], got_shares.at[k], (ps_ss, ps_rs), k, (to, c))
+
+    def sum_copy(k):
+        return remote(sums.at[0], sums.at[k], (pc_ss, pc_rs), k, (r, lax.rem(c + k, n_col)))
+
+    def product_copy(k):
+        return remote(products.at[0], products.at[k], (pp_ss, pp_rs), k, (lax.rem(r + k, n_row), c))
 
     def corner_copies(d):
         n = 2 * RATES.index(d)
@@ -196,9 +190,11 @@
         for copy in inner_copies(d):
             copy().start()
 
-    def own_pack(d):
+    def own_arrive(d):
         for copy in inner_copies(d):
             copy().wait_recv()
+
+    def own_pack(d):
         high = up8(d)
         at = d + (1 - core) * (COLS - d)
         row = lax.broadcasted_iota(jnp.int32, (d, high, BR), 1)
@@ -213,7 +209,6 @@
         side_copies(d)[1]().start()
 
     def outer_side(d):
-        arrive_rows(corner_copies(d))
         at = core * (COLS + d)
         for k in range(0, d, 6):
             SO[d][ROWS * k : ROWS * (k + 6)] = summed(d, at + k, 6, (GCU, GCD), k).astype(BF)
@@ -223,110 +218,157 @@
             side_copies(d)[0]().start()
 
     def own_in(d):
-        arrive_rows(own_copies(d))
         for k in range(0, COLS, 4):
             at = BASE[d] + PLANE[d] + d + k
             z[at : at + 4] = summed(d, d + k, 4, (GHU, GHD), k).reshape(4, ROWS, BR)
 
+    def pixel_sum():
+        for k in range(lanes):
+            acc = jnp.zeros((8, BR), F32)
+            for at in range(0, PIX, 16):
+                rows = x[at : at + 16, BR * k : BR * k + BR].astype(F32)
+                acc = acc + (rows[0:8] + rows[8:16])
+            n, at = divmod(BR * k, share)
+            shares[n, :, at : at + BR] = jnp.sum(acc, axis=0, keepdims=True)
+
     def pool_first():
         for k in range(1, n_row):
-            pool_row(k).start()
+            share_copy(k).start()
 
     def pool_second():
         for k in range(1, n_row):
-            pool_row(k).wait_recv()
-        acc = prow[0]
-        for k in range(1, n_row):
-            acc = acc + prow[k]
-        pcol[0] = acc
+            share_copy(k).wait_recv()
+        acc = shares[r]
+        for k in range(1, n_row):
+            acc = acc + got_shares[k]
+        sums[0] = acc
         for k in range(1, n_col):
-            pool_col(k).start()
+            sum_copy(k).start()
 
     def pool_third():
         for k in range(1, n_col):
-            pool_col(k).wait_recv()
-        acc = pcol[0]
+            sum_copy(k).wait_recv()
+        acc = sums[0]
         for k in range(1, n_col):
-            acc = acc + pcol[k]
+            acc = acc + sums[k]
         pooled = (acc / (PIX * n_row * n_col)).astype(BF).astype(F32)
-        side = jnp.transpose(pooled, (1, 0))
         parts = jnp.zeros((8, BR), F32)
-        for k in range(lanes):
-            prod = side[:, k : k + 1] * wpool[BR * k : BR * k + BR].astype(F32)
-            parts = parts + jnp.sum(prod.reshape(BR // 8, 8, BR), axis=0)
-        branch = jnp.maximum(jnp.sum(parts, axis=0, keepdims=True), 0.0)
-        branch = jnp.broadcast_to(branch, (16, BR)).astype(BF)
+        for k in range(share // BR):
+            side = jnp.transpose(jnp.broadcast_to(pooled[:, BR * k : BR * k + BR], (8, BR)), (1, 0))[:, 0:1]
+            rows = wpool[pl.ds(pl.multiple_of(r * share + BR * k, BR), BR)]
+            parts = parts + jnp.sum((side * rows.astype(F32)).reshape(BR // 8, 8, BR), axis=0)
+        products[0] = jnp.sum(parts, axis=0, keepdims=True)
+        for k in range(1, n_row):
+            product_copy(k).start()
+
+    def pool_fourth():
+        for k in range(1, n_row):
+            product_copy(k).wait_recv()
+        acc = products[0]
+        for k in range(1, n_row):
+            acc = acc + products[k]
+        branch = jnp.broadcast_to(jnp.maximum(acc, 0.0), (16, BR)).astype(BF)
         return jnp.dot(branch, wproj[4 * BR : 5 * BR], preferred_element_type=F32)[0:1]
 
     filled = set()
 
     def put(at, y):
-        y = y.reshape(COLS, ROWS, BR)
+        cols = y.shape[0] // ROWS
+        y = y.reshape(cols, ROWS, BR)
         k = 0
-        while k < COLS:
+        while k < cols:
             old = at + k in filled
             n = 1
-            while k + n < COLS and (at + k + n in filled) == old:
+            while k + n < cols and (at + k + n in filled) == old:
                 n += 1
             if old:
                 z[at + k : at + k + n] += y[k : k + n]
             else:
                 z[at + k : at + k + n] = y[k : k + n]
             k += n
-        filled.update(range(at, at + COLS))
-
-    def multiply(step):
+        filled.update(range(at, at + cols))
+
+    def weights_in(step):
         pltpu.make_async_copy(w.at[step], w.at[step], wsem.at[step]).wait()
-        if step + 3 < STEPS:
-            start_weights(step + 3)
-        if step == 3:
+        if 0 < step < STEPS - 2:
+            start_weights(step + 2)
+        if step == 2:
             for copy in late:
                 copy.start()
+
+    def multiply(step, first=None):
         taps = jnp.concatenate([w[step, k] for k in range(TAPS)], axis=1)
         half = PIX // 2
-        y = jnp.concatenate(
-            [jnp.dot(x[at : at + half], taps, preferred_element_type=F32) for at in (0, half)], axis=0)
-        for k, tap in enumerate(taps_of(step)):
+        if first is None:
+            y = jnp.concatenate(
+                [jnp.dot(x[at : at + half], taps, preferred_element_type=F32) for at in (0, half)], axis=0)
+        else:
+            y = jnp.dot(x[first : first + half], taps, preferred_element_type=F32)
+        for k, tap in enumerate(ORDER[step]):
             at = POINT
             if tap is not None:
                 d, a, b = tap
                 at = BASE[d] + a * PLANE[d] + (2 - b) * d
-            put(at, y[:, BR * k : BR * k + BR])
+            put(at + (first or 0) // ROWS, y[:, BR * k : BR * k + BR])
 
     hole = BASE[18] + PLANE[18] + COLS
     z[hole : hole + 36 - COLS] = jnp.zeros((36 - COLS, ROWS, BR), F32)
     filled.update(range(hole, hole + 36 - COLS))
 
-    multiply(0)
+    xcopies[0].wait()
+    weights_in(0)
+    start_weights(1)
+    multiply(0, 0)
+    xcopies[1].wait()
+    start_weights(2)
+    pixel_sum()
+    multiply(0, PIX // 2)
     pl.semaphore_wait(barrier, n_row + n_col - 2)
+    weights_in(1)
+    pool_first()
     corners_out(18)
-    pool_first()
     multiply(1)
+    own_arrive(18)
+    weights_in(2)
     own_pack(18)
+    start_rows(own_copies(18))
+    multiply(2)
+    pool_second()
+    arrive_rows(corner_copies(18))
+    weights_in(3)
+    corners_out(12)
+    outer_side(18)
     inner_side(18)
-    multiply(2)
-    corners_out(12)
-    start_rows(own_copies(18))
-    outer_side(18)
-    pool_second()
     multiply(3)
-    own_pack(12)
-    inner_side(12)
-    start_rows(own_copies(12))
+    weights_in(4)
+    corners_out(6)
     multiply(4)
-    corners_out(6)
-    outer_side(12)
-    multiply(5)
-    own_pack(6)
-    inner_side(6)
-    outer_side(6)
-    start_rows(own_copies(6))
-    multiply(6)
     for copy in late:
         copy.wait()
-    for d in RATES:
-        own_in(d)
-    pool_part = pool_third()
+    pool_third()
+    own_arrive(12)
+    arrive_rows(corner_copies(12))
+    weights_in(5)
+    outer_side(12)
+    own_pack(12)
+    start_rows(own_copies(12))
+    inner_side(12)
+    arrive_rows(own_copies(18))
+    own_in(18)
+    multiply(5)
+    own_arrive(6)
+    arrive_rows(corner_copies(6))
+    weights_in(6)
+    own_pack(6)
+    start_rows(own_copies(6))
+    outer_side(6)
+    inner_side(6)
+    multiply(6)
+    arrive_rows(own_copies(12))
+    own_in(12)
+    arrive_rows(own_copies(6))
+    own_in(6)
+    pool_part = pool_fourth()
     joined[:, 0:BR] = jnp.maximum(z[POINT : POINT + COLS], 0.0).reshape(PIX, BR).astype(BF)
 
     for n, d in ((3, 18), (2, 12), (1, 6)):
@@ -347,9 +389,10 @@
         out_ref[rows] = jnp.maximum(mixed + pool_part, 0.0).astype(BF)
 
     for k in range(1, n_row):
-        pool_row(k).wait_send()
+        share_copy(k).wait_send()
+        product_copy(k).wait_send()
     for k in range(1, n_col):
-        pool_col(k).wait_send()
+        sum_copy(k).wait_send()
     for d in RATES:
         inner_copies(d)[0]().wait_send()
         inner_copies(d)[1]().wait_send()
@@ -365,7 +408,6 @@
 
 def per_device(n_row, n_col, features, w_point, w_rate_six, w_rate_twelve, w_rate_eighteen, w_pool, w_proj):
     chans = features.shape[2]
-    lanes = chans // BR
     vm = pltpu.VMEM
     dma = pltpu.SemaphoreType.DMA
     scratch = [vm((PIX, chans), BF), vm((STEPS, TAPS, chans, BR), BF), vm((chans, BR), BF), vm((5 * BR, OUT), BF)]
@@ -375,9 +417,10 @@
             scratch += [vm((size(d), BR), BF) for d in RATES]
     for _ in range(2):
         scratch += [vm((d, up8(d), BR), F32) for d in RATES]
-    scratch += [vm((n_row, lanes, BR), F32), vm((n_col, lanes, BR), F32)]
+    share = chans // n_row
+    scratch += [vm((n_row, 1, share), F32), vm((n_row, 1, share), F32), vm((n_col, 1, share), F32), vm((n_row, 1, BR), F32)]
     scratch += [dma((XPARTS,)), dma((STEPS,)), dma((2,))] + [dma((6,))] * 8
-    scratch += [dma((n_row,)), dma((n_row,)), dma((n_col,)), dma((n_col,))]
+    scratch += [dma((n_row,)), dma((n_row,)), dma((n_col,)), dma((n_col,)), dma((n_row,)), dma((n_row,))]
     pixels = jnp.transpose(features, (1, 0, 2)).reshape(PIX, chans)
     out = pl.pallas_call(
         functools.partial(body, n_row, n_col),

time: 29.2 us -> 28.2 us (0.966)
  the two profiles are of different devices: /device:TPU:25 before, /device:TPU:9 now
where the time goes in v4:
time: 28.2 us; the launch traced here: 28.1 us
  Pallas kernels  27.3 us (97%)
  local copies, waits for them, and re-layouts  0.75 us (3%)
    pallas_call x1, Pallas kernels, per_device(): pl.pallas_call(functools.partial(body, n_row, n_col), name='aspp_branches...  27.3 us
    unnamed x1, local copies, waits for them, and re-layouts  0.75 us

profile of v4, /device:TPU:9, one launch (start us, length us, event | category | flops | bytes accessed | tf_op | source)
XLA Modules:
  0.0 28.1 jit_solution(8311645218866003518)
XLA Ops:
  0.0 27.3 %aspp_branches.1 = bf16[800,256]{1,0:T(8,128)(2,1)S(1)} custom-call(bf16[800,2048]{1,0:T(8,128)(2,1)} %bitcast.7, bf16[2048,128]{1,0:T(8,128)(2,1)} %wp_hbm.1, bf16[3,3,2048,128]{3,2,1,0:T(8,128)(2,1)} %w6_hbm.1, bf16[3,3,2048,128]{3,2,1,0:T(8,128)(2,1)} %w12_hbm.1, bf16[3,3,2048,128]{3,2,1,0:T(8,128)(2,1)} %w18_hbm.1, bf16[2048,128]{1,0:T(8,128)(2,1)} %wpool_hbm.1, ...), custom_call_target="tpu_custom_call" | custom-call | flops 11744051200 | bytes 20971520 | tf_op jit(solution)/shard_map/aspp_branches/pallas_call | solution.py:425
  27.3 0.8 %copy.9 = bf16[40,20,256]{2,0,1:T(8,128)(2,1)} copy(bf16[40,20,256]{2,0,1:T(8,128)(2,1)S(1)} %bitcast.6) | data formatting | bytes 819200

commit v5 on v4

--- a/solution.py
+++ b/solution.py
@@ -336,16 +336,13 @@
     pool_second()
     arrive_rows(corner_copies(18))
     weights_in(3)
+    weights_in(4)
     corners_out(12)
     outer_side(18)
     inner_side(18)
     multiply(3)
-    weights_in(4)
     corners_out(6)
     multiply(4)
-    for copy in late:
-        copy.wait()
-    pool_third()
     own_arrive(12)
     arrive_rows(corner_copies(12))
     weights_in(5)
@@ -356,6 +353,9 @@
     arrive_rows(own_copies(18))
     own_in(18)
     multiply(5)
+    for copy in late:
+        copy.wait()
+    pool_third()
     own_arrive(6)
     arrive_rows(corner_copies(6))
     weights_in(6)

time: 28.2 us -> 27.3 us (0.968)
  the two profiles are of different devices: /device:TPU:9 before, /device:TPU:25 now
where the time goes in v5:
time: 27.3 us; the launch traced here: 27.2 us
  Pallas kernels  26.4 us (97%)
  local copies, waits for them, and re-layouts  0.75 us (3%)
    pallas_call x1, Pallas kernels, per_device(): pl.pallas_call(functools.partial(body, n_row, n_col), name='aspp_branches...  26.4 us
    unnamed x1, local copies, waits for them, and re-layouts  0.75 us

profile of v5, /device:TPU:25, one launch (start us, length us, event | category | flops | bytes accessed | tf_op | source)
XLA Modules:
  0.0 27.2 jit_solution(12549336463884650950)
XLA Ops:
  0.0 26.4 %aspp_branches.1 = bf16[800,256]{1,0:T(8,128)(2,1)S(1)} custom-call(bf16[800,2048]{1,0:T(8,128)(2,1)} %bitcast.7, bf16[2048,128]{1,0:T(8,128)(2,1)} %wp_hbm.1, bf16[3,3,2048,128]{3,2,1,0:T(8,128)(2,1)} %w6_hbm.1, bf16[3,3,2048,128]{3,2,1,0:T(8,128)(2,1)} %w12_hbm.1, bf16[3,3,2048,128]{3,2,1,0:T(8,128)(2,1)} %w18_hbm.1, bf16[2048,128]{1,0:T(8,128)(2,1)} %wpool_hbm.1, ...), custom_call_target="tpu_custom_call" | custom-call | flops 11744051200 | bytes 20971520 | tf_op jit(solution)/shard_map/aspp_branches/pallas_call | solution.py:425
  26.4 0.8 %copy.9 = bf16[40,20,256]{2,0,1:T(8,128)(2,1)} copy(bf16[40,20,256]{2,0,1:T(8,128)(2,1)S(1)} %bitcast.6) | data formatting | bytes 819200

commit v6 on v5

--- a/solution.py
+++ b/solution.py
@@ -333,11 +333,11 @@
     own_pack(18)
     start_rows(own_copies(18))
     multiply(2)
+    corners_out(12)
     pool_second()
     arrive_rows(corner_copies(18))
     weights_in(3)
     weights_in(4)
-    corners_out(12)
     outer_side(18)
     inner_side(18)
     multiply(3)

time: 27.3 us -> 27.1 us (level)
  no operation moved by 1% of the time
where the time goes in v6:
time: 27.1 us; the launch traced here: 27 us
  Pallas kernels  26.3 us (97%)
  local copies, waits for them, and re-layouts  0.75 us (3%)
    pallas_call x1, Pallas kernels, per_device(): pl.pallas_call(functools.partial(body, n_row, n_col), name='aspp_branches...  26.3 us
    unnamed x1, local copies, waits for them, and re-layouts  0.75 us

profile of v6, /device:TPU:25, one launch (start us, length us, event | category | flops | bytes accessed | tf_op | source)
XLA Modules:
  0.0 27.0 jit_solution(11211987693465748376)
XLA Ops:
  0.0 26.3 %aspp_branches.1 = bf16[800,256]{1,0:T(8,128)(2,1)S(1)} custom-call(bf16[800,2048]{1,0:T(8,128)(2,1)} %bitcast.7, bf16[2048,128]{1,0:T(8,128)(2,1)} %wp_hbm.1, bf16[3,3,2048,128]{3,2,1,0:T(8,128)(2,1)} %w6_hbm.1, bf16[3,3,2048,128]{3,2,1,0:T(8,128)(2,1)} %w12_hbm.1, bf16[3,3,2048,128]{3,2,1,0:T(8,128)(2,1)} %w18_hbm.1, bf16[2048,128]{1,0:T(8,128)(2,1)} %wpool_hbm.1, ...), custom_call_target="tpu_custom_call" | custom-call | flops 11744051200 | bytes 20971520 | tf_op jit(solution)/shard_map/aspp_branches/pallas_call | solution.py:425
  26.3 0.8 %copy.9 = bf16[40,20,256]{2,0,1:T(8,128)(2,1)} copy(bf16[40,20,256]{2,0,1:T(8,128)(2,1)S(1)} %bitcast.6) | data formatting | bytes 819200
